TPU v7x, 128 devices: a whole 4x4x4 slice. The times are simulated.
128 devices in a mesh: dp: 32 (over x, y, core), space: 4 (over z).
Axes of the slice: x: 4, y: 4, z: 4, core: 2. Of those that a mesh axis runs over, the one named last changes fastest.
Arguments:
- features: bfloat16 [32, 8, 128, 512], P('dp', 'space'), may hold values from -6 to 6
- latent_bank: float32 [1024, 512], replicated, may hold values from -6 to 6
- latent_ids: int32 [32], P('dp'), may hold values from 0 to 1023
- conv_kernel: bfloat16 [3, 3, 512, 512], P(None, None, 'dp'), may hold values from -0.09375 to 0.09375
- style_one: float32 [512, 512], replicated, may hold values from -0.25 to 0.25
- bias_one: float32 [512], replicated, may hold values from 0.1 to 1.9
- style_two: float32 [512, 512], replicated, may hold values from -0.25 to 0.25
- bias_two: float32 [512], replicated, may hold values from 0.1 to 1.9
- rgb_weight: float32 [512, 3], replicated, may hold values from -0.25 to 0.25
- conv_bias: float32 [512], replicated, may hold values from -3 to 3
- direction: float32 [32, 3, 8, 128], P('dp', None, 'space'), may hold values from -60 to 60
- length_target: float32 [1], replicated, may hold values from 0.5 to 3
Outputs:
- kernel_grad: float32 [3, 3, 512, 512], P(None, None, 'dp')
- path_lengths: float32 [32], P('dp')
- new_target: float32 [1], replicated
All inputs are finite; a program needn't handle non-finite values.
Results may differ from a plain program's by a relative error of at most 0.025.
Values may be sent and summed in bfloat16 or wider, within the bound.
No kernel may reach another device: no remote copies, remote signals or barrier semaphores. Data moves between devices by JAX's collectives and lax.ppermute only.
A program may use at most 64 MiB of HBM per device.

v0:
```python
import math
import jax
import jax.numpy as jnp
from jax import lax
from jax.sharding import PartitionSpec as P

PL_WEIGHT = 8.0
PL_DECAY = 0.5
SQRT_TWO = math.sqrt(2.0)
HIGHEST = lax.Precision.HIGHEST


def extended(block, sides, width):
    for axis, dim in sides:
        count = lax.axis_size(axis)
        forward = [(i, i + 1) for i in range(count - 1)]
        backward = [(target, source) for source, target in forward]
        low = lax.ppermute(
            lax.slice_in_dim(block, block.shape[dim] - width, None, axis=dim), axis, forward
        )
        high = lax.ppermute(lax.slice_in_dim(block, 0, width, axis=dim), axis, backward)
        block = jnp.concatenate([low, block, high], axis=dim)
    return block


def synth(padded, latent, kernel_full, params, target_dir, scaling):
    style_one, bias_one, style_two, bias_two, rgb_weight, conv_bias = params
    tile_rows = padded.shape[0] - 2
    tile_cols = padded.shape[1] - 2
    channels = padded.shape[2]
    style_in = jnp.dot(latent, style_one, precision=HIGHEST) + bias_one
    energy = jnp.sum(kernel_full * kernel_full, axis=(0, 1))
    demodulation = lax.rsqrt(jnp.dot(style_in * style_in, energy, precision=HIGHEST) + 1e-08)
    modulated = (
        kernel_full * style_in[None, None, :, None] * demodulation[None, None, None, :]
    ).astype(jnp.bfloat16)
    hidden = jnp.zeros((tile_rows * tile_cols, modulated.shape[3]), jnp.float32) + conv_bias
    for row_off in range(3):
        for col_off in range(3):
            window = padded[row_off : row_off + tile_rows, col_off : col_off + tile_cols].reshape(
                tile_rows * tile_cols, channels
            )
            hidden = hidden + jnp.dot(
                window, modulated[row_off, col_off], preferred_element_type=jnp.float32
            )
    activated = ((0.6 * hidden + 0.4 * jnp.sqrt(hidden * hidden + 0.25)) * SQRT_TWO).astype(
        jnp.bfloat16
    )
    colour = jnp.dot(latent, style_two, precision=HIGHEST) + bias_two
    rgb_mod = (rgb_weight * colour[:, None]).astype(jnp.bfloat16)
    picture = jnp.dot(activated, rgb_mod, preferred_element_type=jnp.float32)
    return jnp.sum(picture * target_dir.reshape(3, tile_rows * tile_cols).T) * scaling


def per_device(
    features,
    latent_bank,
    latent_ids,
    conv_kernel,
    style_one,
    bias_one,
    style_two,
    bias_two,
    rgb_weight,
    conv_bias,
    direction,
    length_target,
):
    kernel_whole = lax.all_gather(conv_kernel, "dp", axis=2, tiled=True)
    kernel_full = kernel_whole.astype(jnp.float32)
    bordered = extended(features, (("space", 1),), 1)
    padded = jnp.pad(bordered, ((0, 0), (0, 0), (1, 1), (0, 0)))
    latents = jnp.take(latent_bank, latent_ids, axis=0)
    scaling = 1.0 / math.sqrt(features.shape[1] * lax.axis_size("space") * features.shape[2])
    params = (style_one, bias_one, style_two, bias_two, rgb_weight, conv_bias)

    def one_grad(pad_one, latent, dir_one):
        return jax.grad(synth, argnums=1)(pad_one, latent, kernel_full, params, dir_one, scaling)

    partial_grads = jax.vmap(one_grad)(padded, latents, direction)
    style_grads = lax.psum(partial_grads, "space")
    lengths = jnp.sqrt(jnp.sum(style_grads * style_grads, axis=1) + 1e-08)
    total = lax.psum(jnp.sum(lengths), "dp")
    target = length_target + PL_DECAY * (
        total / (lengths.shape[0] * lax.axis_size("dp")) - length_target
    )
    factor = 2.0 * PL_WEIGHT * (lengths - target) / lengths
    tangents = factor[:, None] * style_grads

    def total_of(kernel_var):

        def along(pad_one, latent, tangent, dir_one):
            return jax.jvp(
                lambda point: synth(pad_one, point, kernel_var, params, dir_one, scaling),
                (latent,),
                (tangent,),
            )[1]

        return jnp.sum(jax.vmap(along)(padded, latents, tangents, direction))

    kernel_sum = jax.grad(total_of)(kernel_full)
    shard_sum = lax.psum_scatter(
        kernel_sum.astype(jnp.bfloat16), "dp", scatter_dimension=2, tiled=True
    )
    kernel_grad = lax.psum(shard_sum, "space").astype(jnp.float32)
    return (kernel_grad, lengths, target)


def solution(mesh):
    in_specs = (
        P("dp", "space", None, None),
        P(),
        P("dp"),
        P(None, None, "dp", None),
        P(),
        P(),
        P(),
        P(),
        P(),
        P(),
        P("dp", None, "space", None),
        P(),
    )
    out_specs = (P(None, None, "dp", None), P("dp"), P())
    return jax.shard_map(
        per_device, mesh=mesh, in_specs=in_specs, out_specs=out_specs, check_vma=False
    )
```

profile of v0, /device:TPU:0, one launch (start us, length us, event | category | flops | bytes accessed | tf_op | source)
XLA Modules:
  0.0 311.9 jit_solution(5924090728413507393)
XLA Ops:
  7.2 0.7 all-gather.2.cloned.1.call-update
  8.0 1.0 fusion.108
  9.0 3.9 %collective-permute-start = (bf16[1,1,128,512]{3,2,1,0:T(8,128)(2,1)S(1)}, bf16[1,1,128,512]{3,2,1,0:T(8,128)(2,1)S(1)}, u32[]{:S(2)}, u32[]{:S(2)}) collective-permute-start(bf16[1,1,128,512]{3,2,1,0:T(8,128)(2,1)S(1)} %get-tuple-element.29), channel_id=1, source_target_pairs={{0,1},{1,2},{2,3},{4,5},{5,6},{6,7},{8,9},{9,10},{10,11},{12,13},{... | collective-permute-start | bytes 393224 | tf_op jit(solution)/shard_map/ppermute | solution.py:18
  12.9 1.3 collective-permute-start.1
  14.8 1.3 fusion.100
  16.2 0.7 add.176
  16.9 0.7 broadcast_multiply_fusion
  17.5 1.8 fusion.49
  19.3 1.8 fusion.102
  21.2 0.7 fusion.106
  21.9 1.8 pad_maximum_fusion
  23.7 1.1 fusion.61
  24.8 1.0 fusion.107
  25.8 33.8 %all-gather.2.cloned.1.call-done = bf16[3,3,512,512]{3,2,1,0:T(8,128)(2,1)} async-done(((bf16[3,3,16,512]{3,2,1,0:T(8,128)(2,1)}), bf16[3,3,512,512]{3,2,1,0:T(8,128)(2,1)}) %all-gather.2.cloned.1.call-update) | async-done | bytes 4718608 | tf_op jit(solution)/shard_map/all_gather | solution.py:69
  59.6 3.5 %fusion.19 = f32[512,512]{1,0:T(8,128)S(1)} fusion(bf16[3,3,512,512]{3,2,1,0:T(8,128)(2,1)} %all-gather.2.cloned.1.call-done), kind=kLoop, calls=%fused_computation.31 | loop fusion | flops 6815744 | bytes 5767168 | tf_op jit(solution)/shard_map/jvp(vmap(jvp()))/reduce_sum | solution.py:32
  63.1 0.6 fusion.109
  63.8 1.3 fusion.20
  65.7 0.3 fusion.69
  66.3 0.3 convolution_add_fusion.7
  66.7 0.3 fusion.48
  67.0 0.3 convolution_add_fusion.5
  67.3 0.3 fusion.42
  67.6 0.6 multiply_add_fusion.1
  68.2 0.3 fusion.22
  68.6 0.3 fusion.24
  68.9 0.3 fusion.25
  69.3 0.3 fusion.27
  69.6 0.3 fusion.23
  70.0 0.3 fusion.28
  70.3 0.3 fusion.29
  70.7 0.3 fusion.26
  71.0 0.3 fusion.30
  71.4 5.6 %fusion.17 = (f32[512]{0:T(512)S(1)}, f32[512]{0:T(512)S(1)}, bf16[1,3,3,512,512]{4,3,2,1,0:T(8,128)(2,1)}) fusion(bf16[3,3,512,512]{3,2,1,0:T(8,128)(2,1)S(1)} %copy-done.1, f32[512]{0:T(512)S(1)} %get-tuple-element.20, f32[512]{0:T(512)S(1)} %add_rsqrt_fusion, bf16[1,1,1,512,512]{4,3,2,1,0:T(8,128)(2,1)S(1)} %fusion.30, ...), kind=kLoop, calls=%fused_computation.29 | loop fusion | flops 37747712 | bytes 14163968 | tf_op jit(solution)/shard_map/vmap(transpose(jvp()))/reduce_sum | solution.py:35
  77.0 1.0 fusion.111
  78.0 1.0 fusion.112
  79.0 0.4 fusion.56
  79.4 1.0 fusion.110
  80.3 10.7 %psum.21 = f32[1,512]{1,0:T(1,128)S(1)} all-reduce(f32[1,512]{1,0:T(1,128)S(1)} %bitcast.414), channel_id=1, replica_groups=mesh['dp'=32,'space'=4] {'space'}, use_global_device_ids=true, to_apply=%region_4.5 | all-reduce | flops 512 | bytes 4096 | tf_op jit(solution)/shard_map/psum | solution.py:81
  91.0 0.6 multiply_reduce_fusion
  93.0 64.2 %psum.22 = f32[]{:T(128)} all-reduce(f32[]{:T(128)} %sqrt.12), channel_id=1, replica_groups=mesh['dp'=32,'space'=4] {'dp'}, use_global_device_ids=true, to_apply=%region_6.7 | all-reduce | flops 1 | bytes 8 | tf_op jit(solution)/shard_map/psum | solution.py:83
  157.9 0.6 fusion.88
  158.5 0.6 fusion.90
  159.1 0.6 fusion.113
  159.8 4.7 %fusion.21 = bf16[1,3,3,512,512]{4,3,2,1,0:T(8,128)(2,1)S(1)} fusion(bf16[3,3,512,512]{3,2,1,0:T(8,128)(2,1)} %all-gather.2.cloned.1.call-done, f32[512]{0:T(512)S(1)} %fusion.104, f32[512]{0:T(512)S(1)} %bitcast.396, f32[512]{0:T(512)S(1)} %add_rsqrt_fusion, f32[512]{0:T(512)S(1)} %get-tuple-element.20), kind=kLoop, calls=%fused_computation.33 | loop fusion | flops 16515072 | bytes 9445376 | tf_op jit(solution)/shard_map/jvp(vmap(jvp()))/convert_element_type | solution.py:36
  165.4 0.3 fusion.63
  166.0 0.3 convolution_add_fusion.3
  166.3 0.3 convolution_add_fusion.2
  166.7 0.3 convolution_add_fusion.1
  167.0 0.3 fusion.45
  167.3 0.8 fusion.62
  168.1 0.4 fusion.31
  168.5 0.4 fusion.33
  168.8 0.4 fusion.34
  169.2 0.3 fusion.36
  169.5 0.3 fusion.32
  169.9 0.3 fusion.37
  170.2 0.4 fusion.38
  170.6 0.4 fusion.35
  170.9 0.4 fusion.39
  171.4 3.1 fusion.14
  174.7 5.6 %fusion.16 = bf16[3,3,512,512]{3,2,1,0:T(8,128)(2,1)} fusion(bf16[1,3,3,512,512]{4,3,2,1,0:T(8,128)(2,1)S(1)} %bitcast.354, bf16[3,3,512,512]{3,2,1,0:T(8,128)(2,1)S(1)} %bitcast.352, f32[512,512]{1,0:T(8,128)S(1)} %multiply_add_fusion, f32[512]{0:T(512)S(1)} %get-tuple-element.20, f32[512]{0:T(512)S(1)} %fusion.104, f32[512]{0:T(512)S(1)} %bitcast.398, ...), kind=kLoop, calls=%fused_computation.28 | loop fusion | flops 51904512 | bytes 19931136 | tf_op jit(solution)/shard_map/convert_element_type | solution.py:103
  180.3 77.7 %reduce-scatter.2.cloned.1.call-done = bf16[3,3,16,512]{3,2,1,0:T(8,128)(2,1)} async-done(((bf16[3,3,512,512]{3,2,1,0:T(8,128)(2,1)}), bf16[3,3,16,512]{3,2,1,0:T(8,128)(2,1)}) %reduce-scatter.2.cloned.1.call-update) | async-done | bytes 147472 | tf_op jit(solution)/shard_map/reduce_scatter | solution.py:102
  258.1 43.3 %all-reduce.21.cloned.1.call-done = bf16[3,3,16,512]{3,2,1,0:T(8,128)(2,1)} async-done(((bf16[3,3,16,512]{3,2,1,0:T(8,128)(2,1)}), bf16[3,3,16,512]{3,2,1,0:T(8,128)(2,1)}) %all-reduce.21.cloned.1.call-update) | async-done | bytes 147472 | tf_op jit(solution)/shard_map/psum | solution.py:105
  301.4 1.7 convert_element_type.320
  (84 shorter events, 2.6 us)
Async XLA Ops:
  7.2 7.7 %copy-start = (f32[512,512]{1,0:T(8,128)S(1)}, f32[512,512]{1,0:T(8,128)}, u32[]{:S(2)}) copy-start(f32[512,512]{1,0:T(8,128)} %param.18) | copy-start | bytes 3145732
  7.2 52.4 %all-gather.2.cloned.1.call-start = ((), (), s32[]{:S(2)}) async-start(), calls=%async_computation.1 | async-start | bytes 4866048 | tf_op jit(solution)/shard_map/all_gather | solution.py:69
  7.9 250.1 %reduce-scatter.2.cloned.1.call-start = ((), (), s32[]{:S(2)}) async-start(), calls=%async_computation.2 | async-start | bytes 4866048 | tf_op jit(solution)/shard_map/reduce_scatter | solution.py:102
  9.0 12.9 %collective-permute-start = (bf16[1,1,128,512]{3,2,1,0:T(8,128)(2,1)S(1)}, bf16[1,1,128,512]{3,2,1,0:T(8,128)(2,1)S(1)}, u32[]{:S(2)}, u32[]{:S(2)}) collective-permute-start(bf16[1,1,128,512]{3,2,1,0:T(8,128)(2,1)S(1)} %get-tuple-element.29), channel_id=1, source_target_pairs={{0,1},{1,2},{2,3},{4,5},{5,6},{6,7},{8,9},{9,10},{10,11},{12,13},{... | collective-permute-start | bytes 393224 | tf_op jit(solution)/shard_map/ppermute | solution.py:18
  12.9 9.0 %collective-permute-start.1 = (bf16[1,1,128,512]{3,2,1,0:T(8,128)(2,1)S(1)}, bf16[1,1,128,512]{3,2,1,0:T(8,128)(2,1)S(1)}, u32[]{:S(2)}, u32[]{:S(2)}) collective-permute-start(bf16[1,1,128,512]{3,2,1,0:T(8,128)(2,1)S(1)} %get-tuple-element.30), channel_id=1, source_target_pairs={{1,0},{2,1},{3,2},{5,4},{6,5},{7,6},{9,8},{10,9},{11,10},{13,12},{... | collective-permute-start | bytes 393224 | tf_op jit(solution)/shard_map/ppermute | solution.py:21
  25.7 43.2 %copy-start.10 = (bf16[1,2,128,512]{3,2,1,0:T(8,128)(2,1)}, bf16[1,2,128,512]{3,2,1,0:T(8,128)(2,1)S(1)}, u32[]{:S(2)}) copy-start(bf16[1,2,128,512]{3,2,1,0:T(8,128)(2,1)S(1)} %get-tuple-element.23) | copy-start | bytes 786436
  25.7 43.5 %copy-start.8 = (bf16[1,2,128,512]{3,2,1,0:T(8,128)(2,1)}, bf16[1,2,128,512]{3,2,1,0:T(8,128)(2,1)S(1)}, u32[]{:S(2)}) copy-start(bf16[1,2,128,512]{3,2,1,0:T(8,128)(2,1)S(1)} %get-tuple-element.21) | copy-start | bytes 786436
  25.7 44.2 %copy-start.6 = (bf16[1,2,128,512]{3,2,1,0:T(8,128)(2,1)}, bf16[1,2,128,512]{3,2,1,0:T(8,128)(2,1)S(1)}, u32[]{:S(2)}) copy-start(bf16[1,2,128,512]{3,2,1,0:T(8,128)(2,1)S(1)} %get-tuple-element.24) | copy-start | bytes 786436
  25.7 45.3 %copy-start.4 = (bf16[1,2,128,512]{3,2,1,0:T(8,128)(2,1)}, bf16[1,2,128,512]{3,2,1,0:T(8,128)(2,1)S(1)}, u32[]{:S(2)}) copy-start(bf16[1,2,128,512]{3,2,1,0:T(8,128)(2,1)S(1)} %get-tuple-element.25) | copy-start | bytes 786436
  59.6 4.1 %copy-start.1 = (bf16[3,3,512,512]{3,2,1,0:T(8,128)(2,1)S(1)}, bf16[3,3,512,512]{3,2,1,0:T(8,128)(2,1)}, u32[]{:S(2)}) copy-start(bf16[3,3,512,512]{3,2,1,0:T(8,128)(2,1)} %all-gather.2.cloned.1.call-done) | copy-start | bytes 14155780
  63.7 1.6 copy-start.12
  63.7 2.3 copy-start.14
  65.0 1.3 copy-start.23
  65.1 1.6 copy-start.16
  65.4 1.9 copy-start.2
  66.0 1.6 copy-start.18
  66.0 1.6 copy-start.20
  68.2 10.8 %copy-start.24 = (f32[256,512]{1,0:T(8,128)}, f32[256,512]{1,0:T(8,128)S(1)}, u32[]{:S(2)}) copy-start(f32[256,512]{1,0:T(8,128)S(1)} %get-tuple-element.32) | copy-start | bytes 1572868
  71.4 6.6 %copy-start.3 = (f32[512,512]{1,0:T(8,128)S(1)}, f32[512,512]{1,0:T(8,128)}, u32[]{:S(2)}) copy-start(f32[512,512]{1,0:T(8,128)} %param.16) | copy-start | bytes 3145732
  71.4 7.6 %copy-start.22 = (f32[512,3]{0,1:T(4,128)S(1)}, f32[512,3]{0,1:T(4,128)}, u32[]{:S(2)}) copy-start(f32[512,3]{0,1:T(4,128)} %param.20) | copy-start | bytes 18436
  159.7 4.7 %copy-start.5 = (bf16[1,2,128,512]{3,2,1,0:T(8,128)(2,1)S(1)}, bf16[1,2,128,512]{3,2,1,0:T(8,128)(2,1)}, u32[]{:S(2)}) copy-start(bf16[1,2,128,512]{3,2,1,0:T(8,128)(2,1)} %copy-done.4) | copy-start | bytes 786436
  159.7 5.0 %copy-start.11 = (bf16[1,2,128,512]{3,2,1,0:T(8,128)(2,1)S(1)}, bf16[1,2,128,512]{3,2,1,0:T(8,128)(2,1)}, u32[]{:S(2)}) copy-start(bf16[1,2,128,512]{3,2,1,0:T(8,128)(2,1)} %copy-done.10) | copy-start | bytes 786436
  159.8 5.3 %copy-start.13 = (bf16[1,2,128,512]{3,2,1,0:T(8,128)(2,1)S(1)}, bf16[1,2,128,512]{3,2,1,0:T(8,128)(2,1)}, u32[]{:S(2)}) copy-start(bf16[1,2,128,512]{3,2,1,0:T(8,128)(2,1)} %get-tuple-element.22) | copy-start | bytes 786436
  159.8 5.6 %copy-start.15 = (bf16[1,2,128,512]{3,2,1,0:T(8,128)(2,1)S(1)}, bf16[1,2,128,512]{3,2,1,0:T(8,128)(2,1)}, u32[]{:S(2)}) copy-start(bf16[1,2,128,512]{3,2,1,0:T(8,128)(2,1)} %get-tuple-element.26) | copy-start | bytes 786436
  164.4 1.6 copy-start.17
  164.5 1.9 copy-start.7
  164.5 2.2 copy-start.9
  165.7 1.6 copy-start.19
  165.7 1.6 copy-start.21
  165.7 1.6 copy-start.25
  167.3 4.0 %slice-start = ((s8[4718592]{0:T(1024)(128)(4,1)}), s8[4194304]{0:T(1024)(128)(4,1)S(1)}, s32[]{:S(2)}) async-start(s8[4718592]{0:T(1024)(128)(4,1)} %bitcast.351), calls=%async_computation.4 | async-start | bytes 8388608
  167.3 4.0 %slice-start.2 = ((s8[4718592]{0:T(1024)(128)(4,1)}), s8[4194304]{0:T(1024)(128)(4,1)S(1)}, s32[]{:S(2)}) async-start(s8[4718592]{0:T(1024)(128)(4,1)} %bitcast.353), calls=%async_computation.6 | async-start | bytes 8388608
  168.1 3.2 %slice-start.1 = ((s8[4718592]{0:T(1024)(128)(4,1)}), s8[524288]{0:T(1024)(128)(4,1)S(1)}, s32[]{:S(2)}) async-start(s8[4718592]{0:T(1024)(128)(4,1)} %bitcast.351), calls=%async_computation.5 | async-start | bytes 1048576
  168.1 3.2 %slice-start.3 = ((s8[4718592]{0:T(1024)(128)(4,1)}), s8[524288]{0:T(1024)(128)(4,1)S(1)}, s32[]{:S(2)}) async-start(s8[4718592]{0:T(1024)(128)(4,1)} %bitcast.353), calls=%async_computation.7 | async-start | bytes 1048576
  180.3 121.2 %all-reduce.21.cloned.1.call-start = ((), (), s32[]{:S(2)}) async-start(), calls=%async_computation.3 | async-start | bytes 294912 | tf_op jit(solution)/shard_map/psum | solution.py:105
Sparse Core Ops, SparseCore 0:
  10.4 49.1 all-gather.1
  180.4 77.6 reduce-scatter.1
  260.5 40.8 all-reduce.20
where the time goes:
time: 312 us
  waiting for transfers between devices  156 us (50%)
  blocking collectives  74.9 us (24%)
  other arithmetic  31.2 us (10%)
  matrix products  23.2 us (7%)
  between operations  19.4 us (6%)
  starting transfers between devices  5.32 us (2%)
    reduce_scatter x1, waiting for transfers between devices, per_device(): lax.psum_scatter(kernel_sum.astype(jnp.bfloat16), 'dp', scatter_dimension...  77.7 us
    psum x1, blocking collectives, per_device(): total = lax.psum(jnp.sum(lengths), 'dp')  64.2 us
    psum x1, waiting for transfers between devices, per_device(): kernel_grad = lax.psum(shard_sum, 'space').astype(jnp.float32)  43.3 us
    all_gather x1, waiting for transfers between devices, per_device(): kernel_whole = lax.all_gather(conv_kernel, 'dp', axis=2, tiled=True)  33.8 us
    dot_general x36, matrix products, synth(): jnp.dot(window, modulated[row_off, col_off], preferred_element_type=jnp.f...  12.3 us
    psum x1, blocking collectives, per_device(): style_grads = lax.psum(partial_grads, 'space')  10.7 us
    reduce_sum x2, other arithmetic, synth(): kernel_full * style_in[None, None, :, None]  8.7 us
  transfers between devices with their start and end apart: 5, of which 3 were waited for; matrix products, arithmetic and copies ran while one was open for 4% of the time, Pallas kernels for 0%

commit v1 on v0

--- a/solution.py
+++ b/solution.py
@@ -66,7 +66,9 @@
     direction,
     length_target,
 ):
-    kernel_whole = lax.all_gather(conv_kernel, "dp", axis=2, tiled=True)
+    kernel_whole = jnp.concatenate(
+        lax.all_to_all(jnp.stack([conv_kernel] * lax.axis_size("dp")), "dp", 0, 0), axis=2
+    )
     kernel_full = kernel_whole.astype(jnp.float32)
     bordered = extended(features, (("space", 1),), 1)
     padded = jnp.pad(bordered, ((0, 0), (0, 0), (1, 1), (0, 0)))

time: 312 us -> 348 us (1.12)
  waiting for transfers between devices: 156 us -> 168 us
  local copies, waits for them, and re-layouts: 2.12 us -> 9.85 us
  starting transfers between devices: 5.32 us -> 12.9 us
  other arithmetic: 31.2 us -> 37 us
    all_to_all x0 -> x1, waiting for transfers between devices: none -> 45.7 us  [per_device(): lax.all_to_all(jnp.stack([conv_kernel] * lax.axis_size('dp')), 'dp', 0, 0)]
    all_gather x1 -> x0, waiting for transfers between devices: 33.8 us -> none  [per_device(): kernel_whole = lax.all_gather(conv_kernel, 'dp', axis=2, tiled=True)]
    all_to_all x0 -> x1, starting transfers between devices: none -> 7.66 us  [per_device(): lax.all_to_all(jnp.stack([conv_kernel] * lax.axis_size('dp')), 'dp', 0, 0)]
    convert_element_type x0 -> x1, other arithmetic: none -> 7.36 us  [per_device(): kernel_full = kernel_whole.astype(jnp.float32)]
    convert_element_type x0 -> x1, local copies, waits for them, and re-layouts: none -> 4.79 us  [per_device(): kernel_full = kernel_whole.astype(jnp.float32)]
    another operation x0 -> x1, local copies, waits for them, and re-layouts: none -> 3.73 us  [per_device(): jnp.stack([conv_kernel] * lax.axis_size('dp'))]
    reduce_sum x2 -> x3, other arithmetic: 8.7 us -> 5.96 us  [synth(): kernel_full * style_in[None, None, :, None]]
  transfers between devices with their start and end apart: 5 -> 5, of which waited for: 3 -> 4; matrix products, arithmetic and copies ran while one was open for 4% -> 2% of each run, Pallas kernels for 0% -> 0%
where the time goes in v1:
time: 348 us; the launch traced here: 347 us
  waiting for transfers between devices  168 us (48%)
  blocking collectives  75.7 us (22%)
  other arithmetic  37 us (11%)
  matrix products  23.2 us (7%)
  between operations  20 us (6%)
  starting transfers between devices  12.9 us (4%)
  local copies, waits for them, and re-layouts  9.85 us (3%)
    reduce_scatter x1, waiting for transfers between devices, per_device(): lax.psum_scatter(kernel_sum.astype(jnp.bfloat16), 'dp', scatter_dimension...  77.8 us
    psum x1, blocking collectives, per_device(): total = lax.psum(jnp.sum(lengths), 'dp')  63.9 us
    all_to_all x1, waiting for transfers between devices, per_device(): lax.all_to_all(jnp.stack([conv_kernel] * lax.axis_size('dp')), 'dp', 0, 0)  45.7 us
    psum x1, waiting for transfers between devices, per_device(): kernel_grad = lax.psum(shard_sum, 'space').astype(jnp.float32)  43.3 us
    dot_general x36, matrix products, synth(): jnp.dot(window, modulated[row_off, col_off], preferred_element_type=jnp.f...  12.3 us
    psum x1, blocking collectives, per_device(): style_grads = lax.psum(partial_grads, 'space')  11.7 us
    convert_element_type x2, other arithmetic, synth(): modulated = (kernel_full * style_in[None, None, :, None] * demodulation[N...  8.93 us
    convert_element_type x1, other arithmetic, per_device(): kernel_sum.astype(jnp.bfloat16)  7.66 us
  transfers between devices with their start and end apart: 5, of which 4 were waited for; matrix products, arithmetic and copies ran while one was open for 2% of the time, Pallas kernels for 0%

profile of v1, /device:TPU:0, one launch (start us, length us, event | category | flops | bytes accessed | tf_op | source)
XLA Modules:
  0.0 347.0 jit_solution(13128364409742609452)
XLA Ops:
  7.2 3.7 %stack.2 = bf16[32,3,3,16,512]{4,3,2,1,0:T(8,128)(2,1)} broadcast(bf16[3,3,16,512]{3,2,1,0:T(8,128)(2,1)} %param.15), dimensions={1,2,3,4} | broadcast | bytes 4866048 | tf_op jit(solution)/shard_map/stack | solution.py:70
  10.9 7.7 %all-to-all-start = ((bf16[32,3,3,16,512]{4,3,2,1,0:T(8,128)(2,1)}), bf16[32,3,3,16,512]{4,3,2,1,0:T(8,128)(2,1)}, u32[]{:S(2)}, u32[]{:S(2)}) async-start(bf16[32,3,3,16,512]{4,3,2,1,0:T(8,128)(2,1)} %stack.2), calls=%async_computation | async-start | bytes 9437184 | tf_op jit(solution)/shard_map/all_to_all | solution.py:70
  18.7 3.8 %collective-permute-start = (bf16[1,1,128,512]{3,2,1,0:T(8,128)(2,1)S(1)}, bf16[1,1,128,512]{3,2,1,0:T(8,128)(2,1)S(1)}, u32[]{:S(2)}, u32[]{:S(2)}) collective-permute-start(bf16[1,1,128,512]{3,2,1,0:T(8,128)(2,1)S(1)} %get-tuple-element.26), channel_id=1, source_target_pairs={{0,1},{1,2},{2,3},{4,5},{5,6},{6,7},{8,9},{9,10},{10,11},{12,13},{... | collective-permute-start | bytes 393224 | tf_op jit(solution)/shard_map/ppermute | solution.py:18
  22.5 1.3 collective-permute-start.1
  24.5 1.3 fusion.90
  25.9 1.1 fusion.39
  27.0 1.3 fusion.92
  28.3 1.6 collective-permute-done.1
  29.9 0.9 pad_maximum_fusion
  31.0 1.0 fusion.97
  31.9 45.7 %all-to-all-done = bf16[32,3,3,16,512]{4,3,2,1,0:T(8,128)(2,1)} async-done(((bf16[32,3,3,16,512]{4,3,2,1,0:T(8,128)(2,1)}), bf16[32,3,3,16,512]{4,3,2,1,0:T(8,128)(2,1)}, u32[]{:S(2)}, u32[]{:S(2)}) %all-to-all-start) | async-done | bytes 4718624 | tf_op jit(solution)/shard_map/all_to_all | solution.py:70
  77.6 3.6 %fusion.8 = f32[32,16,512]{2,1,0:T(8,128)S(1)} fusion(bf16[32,3,3,16,512]{4,3,2,1,0:T(8,128)(2,1)} %all-to-all-done), kind=kLoop, calls=%fused_computation.17 | loop fusion | flops 6815744 | bytes 5767168 | tf_op jit(solution)/shard_map/jvp(vmap(jvp()))/reduce_sum | solution.py:32
  81.1 0.6 fusion.99
  81.7 7.4 %convert_bitcast_fusion = f32[3,3,32,16,512]{4,3,1,0,2:T(8,128)} fusion(bf16[32,3,3,16,512]{4,3,2,1,0:T(8,128)(2,1)} %all-to-all-done), kind=kLoop, calls=%fused_computation.6 | loop fusion | flops 2359296 | bytes 14155776 | tf_op jit(solution)/shard_map/convert_element_type | solution.py:72
  89.1 4.8 %copy.23 = f32[3,3,32,16,512]{4,3,2,1,0:T(8,128)S(1)} copy(f32[3,3,32,16,512]{4,3,1,0,2:T(8,128)} %convert_bitcast_fusion) | data formatting | bytes 18874368 | tf_op jit(solution)/shard_map/convert_element_type | solution.py:72
  93.9 1.6 multiply_convert_fusion
  95.6 0.3 fusion.60
  95.9 0.3 fusion.59
  96.9 0.3 convolution_add_fusion.7
  97.2 0.3 fusion.38
  97.5 0.3 convolution_add_fusion.5
  97.8 0.3 fusion.32
  98.3 0.6 multiply_add_fusion.1
  98.9 0.3 fusion.12
  99.2 0.3 fusion.14
  99.6 0.3 fusion.15
  100.0 0.3 fusion.17
  100.3 0.3 fusion.13
  100.7 0.3 fusion.18
  101.0 0.3 fusion.19
  101.4 0.3 fusion.20
  101.8 0.3 fusion.16
  102.1 2.0 fusion.10
  104.2 2.2 fusion.2
  106.4 1.0 fusion.101
  107.4 1.0 fusion.102
  108.3 0.4 fusion.46
  108.7 1.0 fusion.100
  109.7 11.7 %psum.21 = f32[1,512]{1,0:T(1,128)S(1)} all-reduce(f32[1,512]{1,0:T(1,128)S(1)} %bitcast.403), channel_id=1, replica_groups=mesh['dp'=32,'space'=4] {'space'}, use_global_device_ids=true, to_apply=%region_4.5 | all-reduce | flops 512 | bytes 4096 | tf_op jit(solution)/shard_map/psum | solution.py:83
  121.4 0.6 multiply_reduce_fusion
  123.4 63.9 %psum.22 = f32[]{:T(128)} all-reduce(f32[]{:T(128)} %sqrt.12), channel_id=1, replica_groups=mesh['dp'=32,'space'=4] {'dp'}, use_global_device_ids=true, to_apply=%region_6.7 | all-reduce | flops 1 | bytes 8 | tf_op jit(solution)/shard_map/psum | solution.py:85
  188.0 0.6 fusion.78
  188.6 1.8 fusion.80
  190.5 0.6 fusion.103
  191.1 7.3 %add_convert_fusion = (bf16[1,3,3,512,512]{4,3,2,1,0:T(8,128)(2,1)S(1)}, f32[512]{0:T(512)S(1)}) fusion(f32[1,3,3,512,512]{4,3,2,1,0:T(8,128)} %bitcast.338, f32[512]{0:T(512)S(1)} %fusion.94, f32[512]{0:T(512)S(1)} %bitcast.386, f32[512]{0:T(512)S(1)} %add_rsqrt_fusion, f32[512]{0:T(512)S(1)} %get-tuple-element.15, ...), kind=kLoop, calls=%fused_computation.22 | loop fusion | flops 40107520 | bytes 18884608 | tf_op jit(solution)/shard_map/jvp(vmap(jvp()))/convert_element_type | solution.py:36
  200.0 0.3 convolution_add_fusion.3
  200.4 0.3 convolution_add_fusion.2
  200.7 0.3 convolution_add_fusion.1
  201.0 0.3 fusion.35
  201.3 0.8 fusion.52
  202.1 0.3 fusion.21
  202.4 0.3 fusion.23
  202.8 0.3 fusion.24
  203.1 0.3 fusion.26
  203.5 0.3 fusion.22
  203.8 0.3 fusion.27
  204.2 0.3 fusion.28
  204.5 0.3 fusion.25
  204.9 0.3 fusion.29
  205.3 1.8 fusion.7
  207.4 7.7 %fusion.9 = bf16[3,3,512,512]{3,2,1,0:T(8,128)(2,1)} fusion(f32[3,3,32,16,512]{4,3,2,1,0:T(8,128)S(1)} %bitcast.340, f32[512,512]{1,0:T(8,128)S(1)} %multiply_add_fusion, f32[512]{0:T(512)S(1)} %fusion.94, f32[512]{0:T(512)S(1)} %bitcast.387, f32[512]{0:T(512)S(1)} %add_rsqrt_fusion, f32[512]{0:T(512)S(1)} %get-tuple-element.15, ...), kind=kLoop, calls=%fused_computation.18 | loop fusion | flops 68419584 | bytes 24649728 | tf_op jit(solution)/shard_map/convert_element_type | solution.py:105
  215.2 77.8 %reduce-scatter.2.cloned.1.call-done = bf16[3,3,16,512]{3,2,1,0:T(8,128)(2,1)} async-done(((bf16[3,3,512,512]{3,2,1,0:T(8,128)(2,1)}), bf16[3,3,16,512]{3,2,1,0:T(8,128)(2,1)}) %reduce-scatter.2.cloned.1.call-update) | async-done | bytes 147472 | tf_op jit(solution)/shard_map/reduce_scatter | solution.py:104
  293.0 43.3 %all-reduce.21.cloned.1.call-done = bf16[3,3,16,512]{3,2,1,0:T(8,128)(2,1)} async-done(((bf16[3,3,16,512]{3,2,1,0:T(8,128)(2,1)}), bf16[3,3,16,512]{3,2,1,0:T(8,128)(2,1)}) %all-reduce.21.cloned.1.call-update) | async-done | bytes 147472 | tf_op jit(solution)/shard_map/psum | solution.py:107
  336.2 1.7 convert_element_type.372
  (128 shorter events, 2.9 us)
Async XLA Ops:
  7.2 17.3 %copy-start = (f32[512,512]{1,0:T(8,128)S(1)}, f32[512,512]{1,0:T(8,128)}, u32[]{:S(2)}) copy-start(f32[512,512]{1,0:T(8,128)} %param.18) | copy-start | bytes 3145732
  10.9 7.8 %copy-start.16 = (bf16[1,2,128,512]{3,2,1,0:T(8,128)(2,1)S(1)}, bf16[1,2,128,512]{3,2,1,0:T(8,128)(2,1)}, u32[]{:S(2)}) copy-start(bf16[1,2,128,512]{3,2,1,0:T(8,128)(2,1)} %param.12) | copy-start | bytes 786436
  10.9 14.9 %copy-start.44 = (f32[512]{0:T(512)S(1)}, f32[512]{0:T(512)}, u32[]{:S(2)}) copy-start(f32[512]{0:T(512)} %param.19) | copy-start | bytes 6148
  10.9 14.9 %copy-start.42 = (f32[1,3,2,128]{3,2,1,0:T(2,128)S(1)}, f32[1,3,2,128]{3,2,1,0:T(2,128)}, u32[]{:S(2)}) copy-start(f32[1,3,2,128]{3,2,1,0:T(2,128)} %param.22) | copy-start | bytes 9220
  10.9 14.9 %copy-start.41 = (f32[512,3]{0,1:T(4,128)S(1)}, f32[512,3]{0,1:T(4,128)}, u32[]{:S(2)}) copy-start(f32[512,3]{0,1:T(4,128)} %param.20) | copy-start | bytes 18436
  10.9 16.0 %copy-start.17 = (f32[512,512]{1,0:T(8,128)S(1)}, f32[512,512]{1,0:T(8,128)}, u32[]{:S(2)}) copy-start(f32[512,512]{1,0:T(8,128)} %param.16) | copy-start | bytes 3145732
  10.9 17.4 %copy-start.45 = (f32[512]{0:T(512)S(1)}, f32[512]{0:T(512)}, u32[]{:S(2)}) copy-start(f32[512]{0:T(512)} %param.17) | copy-start | bytes 6148
  10.9 66.6 %all-to-all-start = ((bf16[32,3,3,16,512]{4,3,2,1,0:T(8,128)(2,1)}), bf16[32,3,3,16,512]{4,3,2,1,0:T(8,128)(2,1)}, u32[]{:S(2)}, u32[]{:S(2)}) async-start(bf16[32,3,3,16,512]{4,3,2,1,0:T(8,128)(2,1)} %stack.2), calls=%async_computation | async-start | bytes 9437184 | tf_op jit(solution)/shard_map/all_to_all | solution.py:70
  18.6 274.3 %reduce-scatter.2.cloned.1.call-start = ((), (), s32[]{:S(2)}) async-start(), calls=%async_computation.2 | async-start | bytes 4866048 | tf_op jit(solution)/shard_map/reduce_scatter | solution.py:104
  18.7 9.6 %collective-permute-start = (bf16[1,1,128,512]{3,2,1,0:T(8,128)(2,1)S(1)}, bf16[1,1,128,512]{3,2,1,0:T(8,128)(2,1)S(1)}, u32[]{:S(2)}, u32[]{:S(2)}) collective-permute-start(bf16[1,1,128,512]{3,2,1,0:T(8,128)(2,1)S(1)} %get-tuple-element.26), channel_id=1, source_target_pairs={{0,1},{1,2},{2,3},{4,5},{5,6},{6,7},{8,9},{9,10},{10,11},{12,13},{... | collective-permute-start | bytes 393224 | tf_op jit(solution)/shard_map/ppermute | solution.py:18
  22.5 7.4 %collective-permute-start.1 = (bf16[1,1,128,512]{3,2,1,0:T(8,128)(2,1)S(1)}, bf16[1,1,128,512]{3,2,1,0:T(8,128)(2,1)S(1)}, u32[]{:S(2)}, u32[]{:S(2)}) collective-permute-start(bf16[1,1,128,512]{3,2,1,0:T(8,128)(2,1)S(1)} %get-tuple-element.27), channel_id=1, source_target_pairs={{1,0},{2,1},{3,2},{5,4},{6,5},{7,6},{9,8},{10,9},{11,10},{13,12},{... | collective-permute-start | bytes 393224 | tf_op jit(solution)/shard_map/ppermute | solution.py:21
  31.9 63.7 %copy-start.22 = (bf16[1,2,128,512]{3,2,1,0:T(8,128)(2,1)}, bf16[1,2,128,512]{3,2,1,0:T(8,128)(2,1)S(1)}, u32[]{:S(2)}) copy-start(bf16[1,2,128,512]{3,2,1,0:T(8,128)(2,1)S(1)} %get-tuple-element.21) | copy-start | bytes 786436
  31.9 64.0 %copy-start.28 = (bf16[1,2,128,512]{3,2,1,0:T(8,128)(2,1)}, bf16[1,2,128,512]{3,2,1,0:T(8,128)(2,1)S(1)}, u32[]{:S(2)}) copy-start(bf16[1,2,128,512]{3,2,1,0:T(8,128)(2,1)S(1)} %get-tuple-element.20) | copy-start | bytes 786436
  31.9 64.9 %copy-start.19 = (bf16[1,2,128,512]{3,2,1,0:T(8,128)(2,1)}, bf16[1,2,128,512]{3,2,1,0:T(8,128)(2,1)S(1)}, u32[]{:S(2)}) copy-start(bf16[1,2,128,512]{3,2,1,0:T(8,128)(2,1)S(1)} %get-tuple-element.22) | copy-start | bytes 786436
  31.9 65.6 %copy-start.25 = (bf16[1,2,128,512]{3,2,1,0:T(8,128)(2,1)}, bf16[1,2,128,512]{3,2,1,0:T(8,128)(2,1)S(1)}, u32[]{:S(2)}) copy-start(bf16[1,2,128,512]{3,2,1,0:T(8,128)(2,1)S(1)} %get-tuple-element.18) | copy-start | bytes 786436
  93.9 10.2 %copy-start.1 = (f32[3,3,32,16,512]{4,3,2,1,0:T(8,128)}, f32[3,3,32,16,512]{4,3,2,1,0:T(8,128)S(1)}, u32[]{:S(2)}) copy-start(f32[3,3,32,16,512]{4,3,2,1,0:T(8,128)S(1)} %copy.23) | copy-start | bytes 28311556
  93.9 2.3 copy-start.31
  93.9 2.6 copy-start.33
  95.6 1.3 copy-start.43
  95.6 1.6 copy-start.35
  96.5 1.6 copy-start.37
  96.5 1.7 copy-start.39
  97.8 1.8 copy-start.29
  97.8 2.1 copy-start.26
  98.3 2.4 copy-start.23
  98.9 9.5 %copy-start.46 = (f32[256,512]{1,0:T(8,128)}, f32[256,512]{1,0:T(8,128)S(1)}, u32[]{:S(2)}) copy-start(f32[256,512]{1,0:T(8,128)S(1)} %get-tuple-element.29) | copy-start | bytes 1572868
  98.9 2.5 copy-start.20
  99.9 4.2 %copy-start.2 = (bf16[1,1,1,512,512]{4,3,2,1,0:T(8,128)(2,1)}, bf16[1,1,1,512,512]{4,3,2,1,0:T(8,128)(2,1)S(1)}, u32[]{:S(2)}) copy-start(bf16[1,1,1,512,512]{4,3,2,1,0:T(8,128)(2,1)S(1)} %fusion.15) | copy-start | bytes 1572868
  100.3 3.8 %copy-start.4 = (bf16[1,1,1,512,512]{4,3,2,1,0:T(8,128)(2,1)}, bf16[1,1,1,512,512]{4,3,2,1,0:T(8,128)(2,1)S(1)}, u32[]{:S(2)}) copy-start(bf16[1,1,1,512,512]{4,3,2,1,0:T(8,128)(2,1)S(1)} %fusion.17) | copy-start | bytes 1572868
  100.7 3.5 copy-start.6
  101.0 3.1 copy-start.8
  101.4 2.7 copy-start.10
  101.8 2.4 copy-start.12
  102.1 2.0 copy-start.14
  104.2 3.2 copy-start.18
  191.1 7.4 %copy-start.21 = (bf16[1,2,128,512]{3,2,1,0:T(8,128)(2,1)S(1)}, bf16[1,2,128,512]{3,2,1,0:T(8,128)(2,1)}, u32[]{:S(2)}) copy-start(bf16[1,2,128,512]{3,2,1,0:T(8,128)(2,1)} %copy-done.19) | copy-start | bytes 786436
  191.1 7.7 %copy-start.30 = (bf16[1,2,128,512]{3,2,1,0:T(8,128)(2,1)S(1)}, bf16[1,2,128,512]{3,2,1,0:T(8,128)(2,1)}, u32[]{:S(2)}) copy-start(bf16[1,2,128,512]{3,2,1,0:T(8,128)(2,1)} %copy-done.28) | copy-start | bytes 786436
  191.1 8.0 %copy-start.32 = (bf16[1,2,128,512]{3,2,1,0:T(8,128)(2,1)S(1)}, bf16[1,2,128,512]{3,2,1,0:T(8,128)(2,1)}, u32[]{:S(2)}) copy-start(bf16[1,2,128,512]{3,2,1,0:T(8,128)(2,1)} %get-tuple-element.19) | copy-start | bytes 786436
  191.1 8.3 %copy-start.34 = (bf16[1,2,128,512]{3,2,1,0:T(8,128)(2,1)S(1)}, bf16[1,2,128,512]{3,2,1,0:T(8,128)(2,1)}, u32[]{:S(2)}) copy-start(bf16[1,2,128,512]{3,2,1,0:T(8,128)(2,1)} %get-tuple-element.23) | copy-start | bytes 786436
  198.4 1.6 copy-start.36
  198.4 1.9 copy-start.24
  198.5 2.2 copy-start.27
  199.7 1.6 copy-start.38
  199.7 1.6 copy-start.40
  199.7 1.6 copy-start.47
  200.3 4.9 %slice-start = ((s8[9437184]{0:T(1024)(128)(4,1)}), s8[4194304]{0:T(1024)(128)(4,1)S(1)}, s32[]{:S(2)}) async-start(s8[9437184]{0:T(1024)(128)(4,1)} %bitcast.339), calls=%async_computation.4 | async-start | bytes 8388608
  201.3 3.9 %slice-start.1 = ((s8[9437184]{0:T(1024)(128)(4,1)}), s8[4194304]{0:T(1024)(128)(4,1)S(1)}, s32[]{:S(2)}) async-start(s8[9437184]{0:T(1024)(128)(4,1)} %bitcast.339), calls=%async_computation.5 | async-start | bytes 8388608
  202.4 2.8 slice-start.2
  205.3 2.1 copy-start.3
  205.3 2.1 copy-start.5
  205.3 2.1 copy-start.7
  205.3 2.1 copy-start.9
  205.3 2.1 copy-start.11
  205.3 2.1 copy-start.13
  205.3 2.1 copy-start.15
  215.1 121.1 %all-reduce.21.cloned.1.call-start = ((), (), s32[]{:S(2)}) async-start(), calls=%async_computation.3 | async-start | bytes 294912 | tf_op jit(solution)/shard_map/psum | solution.py:107
Sparse Core Ops, SparseCore 0:
  215.2 77.6 reduce-scatter.1
  295.4 40.8 all-reduce.20
